TPU v7x, 32 devices: a whole 2x2x4 slice. The times are simulated.
32 devices in a mesh: tm: 8 (over z, x), space: 4 (over y, core).
Axes of the slice: x: 2, y: 2, z: 4, core: 2. Of those that a mesh axis runs over, the one named last changes fastest.
Arguments:
- states: float32 [8, 8, 24, 32, 128], P('tm', None, None, 'space'), may hold values from -6 to 6
- bio_matrix: float32 [8, 8], replicated, may hold values from -2 to 2
- uptake_rate: float32 [32, 128], P('space'), may hold values from 0.2 to 1
- mixing: float32 [23, 32, 128], P(None, 'space'), may hold values from 0.3 to 10
- land_sea: int32 [32, 128], P('space'), may hold values 0 or 1
- levels_active: int32 [32, 128], P('space'), may hold values from 1 to 24
Outputs:
- state_grad: float32 [8, 8, 24, 32, 128], P('tm', None, None, 'space')
- rate_grad: float32 [32, 128], P('space')
All inputs are finite; a program needn't handle non-finite values. No bound on the sum of `land_sea` on one device may be relied on, other than what follows from the above.
Results may differ from a plain program's by a relative error of at most 0.0001.
Values sent between devices are 32-bit elements; how exact they have to be, the bound alone decides.
A program may use at most 64 MiB of HBM per device.

v0:
```python
import math

import jax
import jax.numpy as jnp
from jax import lax
from jax.sharding import PartitionSpec as P

TR = 8
K = 24
STEPS = 4


lateral_mix = 0.24
bio_step = 0.25


def with_halo(shard, sides, width):
    for axis, dim in sides:
        count, length = (lax.axis_size(axis), shard.shape[dim])
        up = [(i, (i + 1) % count) for i in range(count - 1)]
        down = [(j, i) for i, j in up]
        last = lax.slice_in_dim(shard, length - width, length, axis=dim)
        leading = lax.slice_in_dim(shard, 0, width, axis=dim)
        before = lax.ppermute(last, axis, up)
        after = lax.ppermute(leading, axis, down)
        shard = jnp.concatenate([before, shard, after], axis=dim)
    return shard


def shifted(block, axis, distance):
    devices = range(lax.axis_size(axis))
    route = [((i - distance) % len(devices), i) for i in devices]
    return lax.ppermute(block, axis, route)


def vertical_factors(wet, mixing):
    couple = mixing * wet[:-1] * wet[1:]
    depth = wet.shape[0]
    pivots = []
    for height in range(depth):
        middle = 1.0 + jnp.zeros_like(wet[0])
        if height > 0:
            middle = middle + couple[height - 1]
        if height < depth - 1:
            middle = middle + couple[height]
        if height > 0:
            middle = middle - couple[height - 1] * couple[height - 1] / pivots[-1]
        pivots.append(middle)
    return (couple, pivots)


def column_solve(rhs, couple, pivots):
    depth = rhs.shape[1]
    sweep = [rhs[:, 0] / pivots[0]]
    for height in range(1, depth):
        sweep.append((rhs[:, height] + couple[height - 1] * sweep[-1]) / pivots[height])
    result = [sweep[depth - 1]]
    for height in range(depth - 2, -1, -1):
        result.append(sweep[height] + couple[height] / pivots[height] * result[-1])
    return jnp.stack(result[::-1], axis=1)


def shift_cols(field):
    zero_col = jnp.zeros(field.shape[:-1] + (1,), field.dtype)
    east_val = jnp.concatenate([field[..., 1:], zero_col], axis=-1)
    west_val = jnp.concatenate([zero_col, field[..., :-1]], axis=-1)
    return (east_val, west_val)


def face_factors(wet_pad):
    wet = wet_pad[:, 1:-1]
    east_val, west_val = shift_cols(wet)
    return (wet * wet_pad[:, 2:], wet * wet_pad[:, :-2], wet * east_val, wet * west_val)


def lateral_flux(field, padded, faces):
    east_val, west_val = shift_cols(field)
    total = faces[0] * (padded[:, :, 2:] - field) + faces[1] * (padded[:, :, :-2] - field)
    total = total + faces[2] * (east_val - field) + faces[3] * (west_val - field)
    return lateral_mix * total


def forward(start, rims, wet, faces, rate, bio_matrix, couple, pivots):
    field = start
    mixes = []
    for step_idx in range(STEPS):
        mixed = jnp.einsum("tu,ukln->tkln", bio_matrix, field, precision=lax.Precision.HIGHEST)
        mixes.append(mixed)
        star = wet * (field + lateral_flux(field, rims(field), faces) + bio_step * rate * mixed)
        field = column_solve(star, couple, pivots)
    return (field, mixes)


def tracer_halo(field):
    return with_halo(field, (("space", 2),), 1)


def per_device(states, bio_matrix, uptake_rate, mixing, land_sea, levels_active):
    own = states[0]
    depth = mixing.shape[0] + 1
    heights = lax.broadcasted_iota(jnp.int32, (depth,) + land_sea.shape, 0)
    wet = ((land_sea[None] == 1) & (heights < levels_active[None])).astype(jnp.float32)
    wet_pad = with_halo(wet, (("space", 1),), 1)
    faces = face_factors(wet_pad)
    couple, pivots = vertical_factors(wet, mixing)
    following = shifted(own, "tm", -1)
    ending, mixes = forward(own, tracer_halo, wet, faces, uptake_rate, bio_matrix, couple, pivots)
    defect = ending - wet * following
    earlier = shifted(defect, "tm", 1)
    lam = defect
    rate_term = jnp.zeros(uptake_rate.shape, jnp.float32)
    for step_idx in range(STEPS - 1, -1, -1):
        lstar = column_solve(lam, couple, pivots)
        rate_term = rate_term + bio_step * jnp.sum(lstar * wet * mixes[step_idx], axis=(0, 1))
        low = wet * lstar
        back_mix = jnp.einsum("tu,tkln->ukln", bio_matrix, low, precision=lax.Precision.HIGHEST)
        lam = low + lateral_flux(low, tracer_halo(low), faces) + bio_step * uptake_rate * back_mix
    state_grad = (lam - earlier)[None]
    scale = 1.0 / math.sqrt(STEPS * TR * K * lax.axis_size("tm"))
    rate_grad = lax.psum(rate_term, "tm") * scale
    return (state_grad, rate_grad)


def solution(mesh):
    return jax.shard_map(
        per_device,
        mesh=mesh,
        in_specs=(
            P("tm", None, None, "space", None),
            P(),
            P("space", None),
            P(None, "space", None),
            P("space", None),
            P("space", None),
        ),
        out_specs=(P("tm", None, None, "space", None), P("space", None)),
        check_vma=False,
    )
```

profile of v0, /device:TPU:0, one launch (start us, length us, event | category | flops | bytes accessed | tf_op | source)
XLA Modules:
  0.0 113.9 jit_solution(12927892156623937596)
XLA Ops:
  0.7 0.7 broadcast_compare_fusion
  1.4 1.3 %collective-permute-start = (f32[24,1,128]{2,1,0:T(1,128)S(1)}, f32[24,1,128]{2,1,0:T(1,128)S(1)}, u32[]{:S(2)}, u32[]{:S(2)}) collective-permute-start(f32[24,1,128]{2,1,0:T(1,128)S(1)} %get-tuple-element.262), channel_id=1, source_target_pairs={{1,0},{2,1},{3,2},{5,4},{6,5},{7,6},{9,8},{10,9},{11,10},{13,12},{... | collective-permute-start | bytes 36872 | tf_op jit(solution)/shard_map/ppermute | solution.py:25
  2.7 3.0 %collective-permute-start.2 = (f32[24,1,128]{2,1,0:T(1,128)S(1)}, f32[24,1,128]{2,1,0:T(1,128)S(1)}, u32[]{:S(2)}, u32[]{:S(2)}) collective-permute-start(f32[24,1,128]{2,1,0:T(1,128)S(1)} %get-tuple-element.263), channel_id=1, source_target_pairs={{0,1},{1,2},{2,3},{4,5},{5,6},{6,7},{8,9},{9,10},{10,11},{12,13},{... | collective-permute-start | bytes 36872 | tf_op jit(solution)/shard_map/ppermute | solution.py:24
  5.7 1.6 %copy.27 = f32[1,8,24,8,128]{4,1,3,2,0:T(8,128)S(1)} copy(f32[1,8,24,8,128]{4,3,2,1,0:T(8,128)} %param.6) | data formatting | bytes 1572864 | tf_op args[0]
  7.3 6.0 %collective-permute-start.10 = (f32[8,24,8,128]{3,0,2,1:T(8,128)S(1)}, f32[8,24,8,128]{3,0,2,1:T(8,128)S(1)}, u32[]{:S(2)}, u32[]{:S(2)}) collective-permute-start(f32[8,24,8,128]{3,0,2,1:T(8,128)S(1)} %bitcast.191), channel_id=1, source_target_pairs={{4,0},{8,4},{12,8},{16,12},{20,16},{24,20},{28,24},{0,28},{5,1},{9... | collective-permute-start | bytes 2359304 | tf_op jit(solution)/shard_map/ppermute | solution.py:33
  13.4 1.3 %collective-permute-start.1 = (f32[8,24,1,128]{3,0,2,1:T(8,128)S(1)}, f32[8,24,1,128]{3,0,2,1:T(8,128)S(1)}, u32[]{:S(2)}, u32[]{:S(2)}) collective-permute-start(f32[8,24,1,128]{3,0,2,1:T(8,128)S(1)} %get-tuple-element.258), channel_id=1, source_target_pairs={{1,0},{2,1},{3,2},{5,4},{6,5},{7,6},{9,8},{10,9},{11,10},{13,12},{... | collective-permute-start | bytes 294920 | tf_op jit(solution)/shard_map/ppermute | solution.py:25
  14.7 3.4 %collective-permute-start.3 = (f32[8,24,1,128]{3,0,2,1:T(8,128)S(1)}, f32[8,24,1,128]{3,0,2,1:T(8,128)S(1)}, u32[]{:S(2)}, u32[]{:S(2)}) collective-permute-start(f32[8,24,1,128]{3,0,2,1:T(8,128)S(1)} %get-tuple-element.259), channel_id=1, source_target_pairs={{0,1},{1,2},{2,3},{4,5},{5,6},{6,7},{8,9},{9,10},{10,11},{12,13},{... | collective-permute-start | bytes 294920 | tf_op jit(solution)/shard_map/ppermute | solution.py:24
  18.1 0.1 fusion.395
  18.2 0.3 fusion.392
  18.5 0.6 copy-done.2
  19.4 0.3 copy-done.4
  19.8 0.1 fusion.91
  19.9 0.3 copy-done.1
  20.2 1.7 %fusion.87 = (f32[8,24,8,128]{3,0,2,1:T(8,128)S(1)}, f32[8,24,8,128]{3,0,2,1:T(8,128)S(1)}) fusion(f32[8,24,8,128]{3,0,2,1:T(8,128)S(1)} %bitcast.194, f32[8,24,1,128]{3,0,2,1:T(8,128)S(1)} %collective-permute-done.3, f32[8,24,1,128]{3,0,2,1:T(8,128)S(1)} %collective-permute-done.1, f32[8,24,8,127]{3,0,2,1:T(8,128)S(1)} %get-tuple-element.257, ...), kind=kOutput, calls=%fused_computation.109 | convolution fusion | flops 22413312 | bytes 5398784 | tf_op jit(solution)/shard_map/tu,ukln->tkln/dot_general | solution.py:87
  21.9 0.4 constant_dynamic-update-slice_fusion.23
  22.7 1.3 %collective-permute-start.4 = (f32[8,24,1,128]{3,0,2,1:T(8,128)S(1)}, f32[8,24,1,128]{3,0,2,1:T(8,128)S(1)}, u32[]{:S(2)}, u32[]{:S(2)}) collective-permute-start(f32[8,24,1,128]{3,0,2,1:T(8,128)S(1)} %get-tuple-element.254), channel_id=1, source_target_pairs={{1,0},{2,1},{3,2},{5,4},{6,5},{7,6},{9,8},{10,9},{11,10},{13,12},{... | collective-permute-start | bytes 294920 | tf_op jit(solution)/shard_map/ppermute | solution.py:25
  24.0 4.3 %collective-permute-start.5 = (f32[8,24,1,128]{3,0,2,1:T(8,128)S(1)}, f32[8,24,1,128]{3,0,2,1:T(8,128)S(1)}, u32[]{:S(2)}, u32[]{:S(2)}) collective-permute-start(f32[8,24,1,128]{3,0,2,1:T(8,128)S(1)} %get-tuple-element.255), channel_id=1, source_target_pairs={{0,1},{1,2},{2,3},{4,5},{5,6},{6,7},{8,9},{9,10},{10,11},{12,13},{... | collective-permute-start | bytes 294920 | tf_op jit(solution)/shard_map/ppermute | solution.py:24
  28.3 0.3 fusion.390
  28.6 0.6 collective-permute-done.5
  29.2 1.3 %fusion.76 = (f32[8,24,8,128]{3,0,2,1:T(8,128)S(1)}, f32[8,24,8,128]{3,0,2,1:T(8,128)S(1)}) fusion(f32[8,24,8,128]{3,0,2,1:T(8,128)S(1)} %constant_dynamic-update-slice_fusion, f32[8,24,1,128]{3,0,2,1:T(8,128)S(1)} %collective-permute-done.5, f32[8,24,1,128]{3,0,2,1:T(8,128)S(1)} %collective-permute-done.4, f32[8,24,8,127]{3,0,2,1:T(8,128)S(1)} %get-tuple-element.253, ...), kind=kOutput, calls=%fused_computation.96 | convolution fusion | flops 22413312 | bytes 4612352 | tf_op jit(solution)/shard_map/tu,ukln->tkln/dot_general | solution.py:87
  30.5 0.4 constant_dynamic-update-slice_fusion.47
  31.2 1.3 %collective-permute-start.6 = (f32[8,24,1,128]{3,0,2,1:T(8,128)S(1)}, f32[8,24,1,128]{3,0,2,1:T(8,128)S(1)}, u32[]{:S(2)}, u32[]{:S(2)}) collective-permute-start(f32[8,24,1,128]{3,0,2,1:T(8,128)S(1)} %get-tuple-element.250), channel_id=1, source_target_pairs={{1,0},{2,1},{3,2},{5,4},{6,5},{7,6},{9,8},{10,9},{11,10},{13,12},{... | collective-permute-start | bytes 294920 | tf_op jit(solution)/shard_map/ppermute | solution.py:25
  32.5 5.1 %collective-permute-start.7 = (f32[8,24,1,128]{3,0,2,1:T(8,128)S(1)}, f32[8,24,1,128]{3,0,2,1:T(8,128)S(1)}, u32[]{:S(2)}, u32[]{:S(2)}) collective-permute-start(f32[8,24,1,128]{3,0,2,1:T(8,128)S(1)} %get-tuple-element.251), channel_id=1, source_target_pairs={{0,1},{1,2},{2,3},{4,5},{5,6},{6,7},{8,9},{9,10},{10,11},{12,13},{... | collective-permute-start | bytes 294920 | tf_op jit(solution)/shard_map/ppermute | solution.py:24
  37.6 0.3 fusion.388
  37.9 0.6 collective-permute-done.7
  38.6 1.3 %fusion.65 = (f32[8,24,8,128]{3,0,2,1:T(8,128)S(1)}, f32[8,24,8,128]{3,0,2,1:T(8,128)S(1)}) fusion(f32[8,24,8,128]{3,0,2,1:T(8,128)S(1)} %constant_dynamic-update-slice_fusion.24, f32[8,24,1,128]{3,0,2,1:T(8,128)S(1)} %collective-permute-done.7, f32[8,24,1,128]{3,0,2,1:T(8,128)S(1)} %collective-permute-done.6, ...), kind=kOutput, calls=%fused_computation.83 | convolution fusion | flops 22413312 | bytes 4612352 | tf_op jit(solution)/shard_map/tu,ukln->tkln/dot_general | solution.py:87
  39.9 0.4 constant_dynamic-update-slice_fusion.71
  40.6 1.3 %collective-permute-start.8 = (f32[8,24,1,128]{3,0,2,1:T(8,128)S(1)}, f32[8,24,1,128]{3,0,2,1:T(8,128)S(1)}, u32[]{:S(2)}, u32[]{:S(2)}) collective-permute-start(f32[8,24,1,128]{3,0,2,1:T(8,128)S(1)} %get-tuple-element.246), channel_id=1, source_target_pairs={{1,0},{2,1},{3,2},{5,4},{6,5},{7,6},{9,8},{10,9},{11,10},{13,12},{... | collective-permute-start | bytes 294920 | tf_op jit(solution)/shard_map/ppermute | solution.py:25
  41.9 5.6 %collective-permute-start.9 = (f32[8,24,1,128]{3,0,2,1:T(8,128)S(1)}, f32[8,24,1,128]{3,0,2,1:T(8,128)S(1)}, u32[]{:S(2)}, u32[]{:S(2)}) collective-permute-start(f32[8,24,1,128]{3,0,2,1:T(8,128)S(1)} %get-tuple-element.247), channel_id=1, source_target_pairs={{0,1},{1,2},{2,3},{4,5},{5,6},{6,7},{8,9},{9,10},{10,11},{12,13},{... | collective-permute-start | bytes 294920 | tf_op jit(solution)/shard_map/ppermute | solution.py:24
  47.5 0.3 fusion.386
  47.8 0.6 collective-permute-done.9
  48.5 1.3 %fusion.54 = (f32[8,24,8,128]{3,0,2,1:T(8,128)S(1)}, f32[8,24,8,128]{3,0,2,1:T(8,128)S(1)}) fusion(f32[8,24,8,128]{3,0,2,1:T(8,128)S(1)} %constant_dynamic-update-slice_fusion.48, f32[8,24,1,128]{3,0,2,1:T(8,128)S(1)} %collective-permute-done.9, f32[8,24,1,128]{3,0,2,1:T(8,128)S(1)} %collective-permute-done.8, ...), kind=kOutput, calls=%fused_computation.70 | convolution fusion | flops 22413312 | bytes 4612352 | tf_op jit(solution)/shard_map/tu,ukln->tkln/dot_general | solution.py:87
  49.8 0.4 constant_dynamic-update-slice_fusion.95
  50.5 0.2 multiply_subtract_fusion
  50.7 0.4 constant_dynamic-update-slice_fusion.119
  51.4 0.2 multiply_reduce_fusion.3
  51.6 1.3 %collective-permute-start.11 = (f32[8,24,1,128]{3,0,2,1:T(8,128)S(1)}, f32[8,24,1,128]{3,0,2,1:T(8,128)S(1)}, u32[]{:S(2)}, u32[]{:S(2)}) collective-permute-start(f32[8,24,1,128]{3,0,2,1:T(8,128)S(1)} %get-tuple-element.242), channel_id=1, source_target_pairs={{1,0},{2,1},{3,2},{5,4},{6,5},{7,6},{9,8},{10,9},{11,10},{13,12},{... | collective-permute-start | bytes 294920 | tf_op jit(solution)/shard_map/ppermute | solution.py:25
  52.9 5.8 %collective-permute-start.12 = (f32[8,24,1,128]{3,0,2,1:T(8,128)S(1)}, f32[8,24,1,128]{3,0,2,1:T(8,128)S(1)}, u32[]{:S(2)}, u32[]{:S(2)}) collective-permute-start(f32[8,24,1,128]{3,0,2,1:T(8,128)S(1)} %get-tuple-element.243), channel_id=1, source_target_pairs={{0,1},{1,2},{2,3},{4,5},{5,6},{6,7},{8,9},{9,10},{10,11},{12,13},{... | collective-permute-start | bytes 294920 | tf_op jit(solution)/shard_map/ppermute | solution.py:24
  58.8 0.3 fusion.384
  59.1 0.4 collective-permute-done.12
  59.5 1.3 %fusion.4 = f32[8,24,8,128]{3,0,2,1:T(8,128)S(1)} fusion(f32[8,24,8,128]{3,0,2,1:T(8,128)S(1)} %get-tuple-element.7, f32[8,24,1,128]{3,0,2,1:T(8,128)S(1)} %collective-permute-done.12, f32[8,24,1,128]{3,0,2,1:T(8,128)S(1)} %collective-permute-done.11, f32[8,24,8,127]{3,0,2,1:T(8,128)S(1)} %get-tuple-element.241, ...), kind=kOutput, calls=%fused_computation.11 | convolution fusion | flops 22216704 | bytes 3727616 | tf_op jit(solution)/shard_map/tu,tkln->ukln/dot_general | solution.py:116
  60.8 0.4 constant_dynamic-update-slice_fusion.143
  61.5 0.2 multiply_reduce_fusion.2
  61.7 1.3 %collective-permute-start.13 = (f32[8,24,1,128]{3,0,2,1:T(8,128)S(1)}, f32[8,24,1,128]{3,0,2,1:T(8,128)S(1)}, u32[]{:S(2)}, u32[]{:S(2)}) collective-permute-start(f32[8,24,1,128]{3,0,2,1:T(8,128)S(1)} %get-tuple-element.238), channel_id=1, source_target_pairs={{1,0},{2,1},{3,2},{5,4},{6,5},{7,6},{9,8},{10,9},{11,10},{13,12},{... | collective-permute-start | bytes 294920 | tf_op jit(solution)/shard_map/ppermute | solution.py:25
  63.0 5.6 %collective-permute-start.14 = (f32[8,24,1,128]{3,0,2,1:T(8,128)S(1)}, f32[8,24,1,128]{3,0,2,1:T(8,128)S(1)}, u32[]{:S(2)}, u32[]{:S(2)}) collective-permute-start(f32[8,24,1,128]{3,0,2,1:T(8,128)S(1)} %get-tuple-element.239), channel_id=1, source_target_pairs={{0,1},{1,2},{2,3},{4,5},{5,6},{6,7},{8,9},{9,10},{10,11},{12,13},{... | collective-permute-start | bytes 294920 | tf_op jit(solution)/shard_map/ppermute | solution.py:24
  68.7 0.3 fusion.382
  69.0 0.6 collective-permute-done.14
  69.6 1.3 %fusion.5 = f32[8,24,8,128]{3,0,2,1:T(8,128)S(1)} fusion(f32[8,24,8,128]{3,0,2,1:T(8,128)S(1)} %get-tuple-element.5, f32[8,24,1,128]{3,0,2,1:T(8,128)S(1)} %collective-permute-done.14, f32[8,24,1,128]{3,0,2,1:T(8,128)S(1)} %collective-permute-done.13, f32[8,24,8,127]{3,0,2,1:T(8,128)S(1)} %get-tuple-element.237, ...), kind=kOutput, calls=%fused_computation.12 | convolution fusion | flops 22216704 | bytes 3727616 | tf_op jit(solution)/shard_map/tu,tkln->ukln/dot_general | solution.py:116
  70.9 0.4 constant_dynamic-update-slice_fusion.167
  71.6 0.2 multiply_reduce_fusion.1
  71.8 1.3 %collective-permute-start.15 = (f32[8,24,1,128]{3,0,2,1:T(8,128)S(1)}, f32[8,24,1,128]{3,0,2,1:T(8,128)S(1)}, u32[]{:S(2)}, u32[]{:S(2)}) collective-permute-start(f32[8,24,1,128]{3,0,2,1:T(8,128)S(1)} %get-tuple-element.234), channel_id=1, source_target_pairs={{1,0},{2,1},{3,2},{5,4},{6,5},{7,6},{9,8},{10,9},{11,10},{13,12},{... | collective-permute-start | bytes 294920 | tf_op jit(solution)/shard_map/ppermute | solution.py:25
  73.1 5.6 %collective-permute-start.16 = (f32[8,24,1,128]{3,0,2,1:T(8,128)S(1)}, f32[8,24,1,128]{3,0,2,1:T(8,128)S(1)}, u32[]{:S(2)}, u32[]{:S(2)}) collective-permute-start(f32[8,24,1,128]{3,0,2,1:T(8,128)S(1)} %get-tuple-element.235), channel_id=1, source_target_pairs={{0,1},{1,2},{2,3},{4,5},{5,6},{6,7},{8,9},{9,10},{10,11},{12,13},{... | collective-permute-start | bytes 294920 | tf_op jit(solution)/shard_map/ppermute | solution.py:24
  78.7 0.3 fusion.380
  79.0 0.6 collective-permute-done.16
  79.7 1.3 %fusion.6 = f32[8,24,8,128]{3,0,2,1:T(8,128)S(1)} fusion(f32[8,24,8,128]{3,0,2,1:T(8,128)S(1)} %get-tuple-element.9, f32[8,24,1,128]{3,0,2,1:T(8,128)S(1)} %collective-permute-done.16, f32[8,24,1,128]{3,0,2,1:T(8,128)S(1)} %collective-permute-done.15, f32[8,24,8,127]{3,0,2,1:T(8,128)S(1)} %get-tuple-element.233, ...), kind=kOutput, calls=%fused_computation.13 | convolution fusion | flops 22216704 | bytes 3727616 | tf_op jit(solution)/shard_map/tu,tkln->ukln/dot_general | solution.py:116
  81.0 0.4 constant_dynamic-update-slice_fusion.191
  81.7 0.2 multiply_reduce_fusion
  81.9 1.3 %collective-permute-start.17 = (f32[8,24,1,128]{3,0,2,1:T(8,128)S(1)}, f32[8,24,1,128]{3,0,2,1:T(8,128)S(1)}, u32[]{:S(2)}, u32[]{:S(2)}) collective-permute-start(f32[8,24,1,128]{3,0,2,1:T(8,128)S(1)} %get-tuple-element.230), channel_id=1, source_target_pairs={{1,0},{2,1},{3,2},{5,4},{6,5},{7,6},{9,8},{10,9},{11,10},{13,12},{... | collective-permute-start | bytes 294920 | tf_op jit(solution)/shard_map/ppermute | solution.py:25
  83.2 5.6 %collective-permute-start.18 = (f32[8,24,1,128]{3,0,2,1:T(8,128)S(1)}, f32[8,24,1,128]{3,0,2,1:T(8,128)S(1)}, u32[]{:S(2)}, u32[]{:S(2)}) collective-permute-start(f32[8,24,1,128]{3,0,2,1:T(8,128)S(1)} %get-tuple-element.231), channel_id=1, source_target_pairs={{0,1},{1,2},{2,3},{4,5},{5,6},{6,7},{8,9},{9,10},{10,11},{12,13},{... | collective-permute-start | bytes 294920 | tf_op jit(solution)/shard_map/ppermute | solution.py:24
  88.8 21.8 %psum.7 = f32[8,128]{1,0:T(8,128)S(1)} all-reduce(f32[8,128]{1,0:T(8,128)S(1)} %add_multiply_fusion), channel_id=1, replica_groups=mesh['tm'=8,'space'=4] {'tm'}, use_global_device_ids=true, to_apply=%region_4.0 | all-reduce | flops 1024 | bytes 8192 | tf_op jit(solution)/shard_map/psum | solution.py:120
  110.6 0.3 fusion.378
  110.9 0.6 broadcast_multiply_fusion.4
  111.5 1.3 %fusion.16 = f32[1,8,24,8,128]{4,1,3,2,0:T(8,128)S(1)} fusion(f32[8,24,8,128]{3,0,2,1:T(8,128)S(1)} %collective-permute-done.19, f32[8,24,8,128]{3,0,2,1:T(8,128)S(1)} %get-tuple-element.11, f32[8,24,1,128]{3,0,2,1:T(8,128)S(1)} %collective-permute-done.18, f32[8,24,1,128]{3,0,2,1:T(8,128)S(1)} %collective-permute-done.17, ...), kind=kOutput, calls=%fused_computation.24 | convolution fusion | flops 22413312 | bytes 4514048 | tf_op jit(solution)/shard_map/tu,tkln->ukln/dot_general | solution.py:116
  112.9 1.0 copy.13
  (232 shorter events, 2.1 us)
Async XLA Ops:
  0.6 19.3 %copy-start = (f32[8,8]{1,0:T(8,128)S(1)}, f32[8,8]{1,0:T(8,128)}, u32[]{:S(2)}) copy-start(f32[8,8]{1,0:T(8,128)} %param.7) | copy-start | bytes 772
  0.6 0.7 copy-start.3
  1.4 18.4 %collective-permute-start = (f32[24,1,128]{2,1,0:T(1,128)S(1)}, f32[24,1,128]{2,1,0:T(1,128)S(1)}, u32[]{:S(2)}, u32[]{:S(2)}) collective-permute-start(f32[24,1,128]{2,1,0:T(1,128)S(1)} %get-tuple-element.262), channel_id=1, source_target_pairs={{1,0},{2,1},{3,2},{5,4},{6,5},{7,6},{9,8},{10,9},{11,10},{13,12},{... | collective-permute-start | bytes 36872 | tf_op jit(solution)/shard_map/ppermute | solution.py:25
  2.7 17.1 %collective-permute-start.2 = (f32[24,1,128]{2,1,0:T(1,128)S(1)}, f32[24,1,128]{2,1,0:T(1,128)S(1)}, u32[]{:S(2)}, u32[]{:S(2)}) collective-permute-start(f32[24,1,128]{2,1,0:T(1,128)S(1)} %get-tuple-element.263), channel_id=1, source_target_pairs={{0,1},{1,2},{2,3},{4,5},{5,6},{6,7},{8,9},{9,10},{10,11},{12,13},{... | collective-permute-start | bytes 36872 | tf_op jit(solution)/shard_map/ppermute | solution.py:24
  7.3 43.1 %collective-permute-start.10 = (f32[8,24,8,128]{3,0,2,1:T(8,128)S(1)}, f32[8,24,8,128]{3,0,2,1:T(8,128)S(1)}, u32[]{:S(2)}, u32[]{:S(2)}) collective-permute-start(f32[8,24,8,128]{3,0,2,1:T(8,128)S(1)} %bitcast.191), channel_id=1, source_target_pairs={{4,0},{8,4},{12,8},{16,12},{20,16},{24,20},{28,24},{0,28},{5,1},{9... | collective-permute-start | bytes 2359304 | tf_op jit(solution)/shard_map/ppermute | solution.py:33
  13.4 6.5 %collective-permute-start.1 = (f32[8,24,1,128]{3,0,2,1:T(8,128)S(1)}, f32[8,24,1,128]{3,0,2,1:T(8,128)S(1)}, u32[]{:S(2)}, u32[]{:S(2)}) collective-permute-start(f32[8,24,1,128]{3,0,2,1:T(8,128)S(1)} %get-tuple-element.258), channel_id=1, source_target_pairs={{1,0},{2,1},{3,2},{5,4},{6,5},{7,6},{9,8},{10,9},{11,10},{13,12},{... | collective-permute-start | bytes 294920 | tf_op jit(solution)/shard_map/ppermute | solution.py:25
  14.7 5.2 %collective-permute-start.3 = (f32[8,24,1,128]{3,0,2,1:T(8,128)S(1)}, f32[8,24,1,128]{3,0,2,1:T(8,128)S(1)}, u32[]{:S(2)}, u32[]{:S(2)}) collective-permute-start(f32[8,24,1,128]{3,0,2,1:T(8,128)S(1)} %get-tuple-element.259), channel_id=1, source_target_pairs={{0,1},{1,2},{2,3},{4,5},{5,6},{6,7},{8,9},{9,10},{10,11},{12,13},{... | collective-permute-start | bytes 294920 | tf_op jit(solution)/shard_map/ppermute | solution.py:24
  18.2 0.9 copy-start.2
  19.1 0.7 copy-start.4
  19.1 1.1 copy-start.1
  22.7 5.9 %collective-permute-start.4 = (f32[8,24,1,128]{3,0,2,1:T(8,128)S(1)}, f32[8,24,1,128]{3,0,2,1:T(8,128)S(1)}, u32[]{:S(2)}, u32[]{:S(2)}) collective-permute-start(f32[8,24,1,128]{3,0,2,1:T(8,128)S(1)} %get-tuple-element.254), channel_id=1, source_target_pairs={{1,0},{2,1},{3,2},{5,4},{6,5},{7,6},{9,8},{10,9},{11,10},{13,12},{... | collective-permute-start | bytes 294920 | tf_op jit(solution)/shard_map/ppermute | solution.py:25
  24.0 5.2 %collective-permute-start.5 = (f32[8,24,1,128]{3,0,2,1:T(8,128)S(1)}, f32[8,24,1,128]{3,0,2,1:T(8,128)S(1)}, u32[]{:S(2)}, u32[]{:S(2)}) collective-permute-start(f32[8,24,1,128]{3,0,2,1:T(8,128)S(1)} %get-tuple-element.255), channel_id=1, source_target_pairs={{0,1},{1,2},{2,3},{4,5},{5,6},{6,7},{8,9},{9,10},{10,11},{12,13},{... | collective-permute-start | bytes 294920 | tf_op jit(solution)/shard_map/ppermute | solution.py:24
  31.2 6.7 %collective-permute-start.6 = (f32[8,24,1,128]{3,0,2,1:T(8,128)S(1)}, f32[8,24,1,128]{3,0,2,1:T(8,128)S(1)}, u32[]{:S(2)}, u32[]{:S(2)}) collective-permute-start(f32[8,24,1,128]{3,0,2,1:T(8,128)S(1)} %get-tuple-element.250), channel_id=1, source_target_pairs={{1,0},{2,1},{3,2},{5,4},{6,5},{7,6},{9,8},{10,9},{11,10},{13,12},{... | collective-permute-start | bytes 294920 | tf_op jit(solution)/shard_map/ppermute | solution.py:25
  32.5 6.0 %collective-permute-start.7 = (f32[8,24,1,128]{3,0,2,1:T(8,128)S(1)}, f32[8,24,1,128]{3,0,2,1:T(8,128)S(1)}, u32[]{:S(2)}, u32[]{:S(2)}) collective-permute-start(f32[8,24,1,128]{3,0,2,1:T(8,128)S(1)} %get-tuple-element.251), channel_id=1, source_target_pairs={{0,1},{1,2},{2,3},{4,5},{5,6},{6,7},{8,9},{9,10},{10,11},{12,13},{... | collective-permute-start | bytes 294920 | tf_op jit(solution)/shard_map/ppermute | solution.py:24
  40.6 7.2 %collective-permute-start.8 = (f32[8,24,1,128]{3,0,2,1:T(8,128)S(1)}, f32[8,24,1,128]{3,0,2,1:T(8,128)S(1)}, u32[]{:S(2)}, u32[]{:S(2)}) collective-permute-start(f32[8,24,1,128]{3,0,2,1:T(8,128)S(1)} %get-tuple-element.246), channel_id=1, source_target_pairs={{1,0},{2,1},{3,2},{5,4},{6,5},{7,6},{9,8},{10,9},{11,10},{13,12},{... | collective-permute-start | bytes 294920 | tf_op jit(solution)/shard_map/ppermute | solution.py:25
  41.9 6.6 %collective-permute-start.9 = (f32[8,24,1,128]{3,0,2,1:T(8,128)S(1)}, f32[8,24,1,128]{3,0,2,1:T(8,128)S(1)}, u32[]{:S(2)}, u32[]{:S(2)}) collective-permute-start(f32[8,24,1,128]{3,0,2,1:T(8,128)S(1)} %get-tuple-element.247), channel_id=1, source_target_pairs={{0,1},{1,2},{2,3},{4,5},{5,6},{6,7},{8,9},{9,10},{10,11},{12,13},{... | collective-permute-start | bytes 294920 | tf_op jit(solution)/shard_map/ppermute | solution.py:24
  50.7 60.9 %collective-permute-start.19 = (f32[8,24,8,128]{3,0,2,1:T(8,128)S(1)}, f32[8,24,8,128]{3,0,2,1:T(8,128)S(1)}, u32[]{:S(2)}, u32[]{:S(2)}) collective-permute-start(f32[8,24,8,128]{3,0,2,1:T(8,128)S(1)} %multiply_subtract_fusion), channel_id=1, source_target_pairs={{28,0},{0,4},{4,8},{8,12},{12,16},{16,20},{20,24},{24,28},{29,1},{... | collective-permute-start | bytes 2359304 | tf_op jit(solution)/shard_map/ppermute | solution.py:33
  51.6 7.4 %collective-permute-start.11 = (f32[8,24,1,128]{3,0,2,1:T(8,128)S(1)}, f32[8,24,1,128]{3,0,2,1:T(8,128)S(1)}, u32[]{:S(2)}, u32[]{:S(2)}) collective-permute-start(f32[8,24,1,128]{3,0,2,1:T(8,128)S(1)} %get-tuple-element.242), channel_id=1, source_target_pairs={{1,0},{2,1},{3,2},{5,4},{6,5},{7,6},{9,8},{10,9},{11,10},{13,12},{... | collective-permute-start | bytes 294920 | tf_op jit(solution)/shard_map/ppermute | solution.py:25
  52.9 6.6 %collective-permute-start.12 = (f32[8,24,1,128]{3,0,2,1:T(8,128)S(1)}, f32[8,24,1,128]{3,0,2,1:T(8,128)S(1)}, u32[]{:S(2)}, u32[]{:S(2)}) collective-permute-start(f32[8,24,1,128]{3,0,2,1:T(8,128)S(1)} %get-tuple-element.243), channel_id=1, source_target_pairs={{0,1},{1,2},{2,3},{4,5},{5,6},{6,7},{8,9},{9,10},{10,11},{12,13},{... | collective-permute-start | bytes 294920 | tf_op jit(solution)/shard_map/ppermute | solution.py:24
  61.7 7.2 %collective-permute-start.13 = (f32[8,24,1,128]{3,0,2,1:T(8,128)S(1)}, f32[8,24,1,128]{3,0,2,1:T(8,128)S(1)}, u32[]{:S(2)}, u32[]{:S(2)}) collective-permute-start(f32[8,24,1,128]{3,0,2,1:T(8,128)S(1)} %get-tuple-element.238), channel_id=1, source_target_pairs={{1,0},{2,1},{3,2},{5,4},{6,5},{7,6},{9,8},{10,9},{11,10},{13,12},{... | collective-permute-start | bytes 294920 | tf_op jit(solution)/shard_map/ppermute | solution.py:25
  63.0 6.6 %collective-permute-start.14 = (f32[8,24,1,128]{3,0,2,1:T(8,128)S(1)}, f32[8,24,1,128]{3,0,2,1:T(8,128)S(1)}, u32[]{:S(2)}, u32[]{:S(2)}) collective-permute-start(f32[8,24,1,128]{3,0,2,1:T(8,128)S(1)} %get-tuple-element.239), channel_id=1, source_target_pairs={{0,1},{1,2},{2,3},{4,5},{5,6},{6,7},{8,9},{9,10},{10,11},{12,13},{... | collective-permute-start | bytes 294920 | tf_op jit(solution)/shard_map/ppermute | solution.py:24
  71.8 7.2 %collective-permute-start.15 = (f32[8,24,1,128]{3,0,2,1:T(8,128)S(1)}, f32[8,24,1,128]{3,0,2,1:T(8,128)S(1)}, u32[]{:S(2)}, u32[]{:S(2)}) collective-permute-start(f32[8,24,1,128]{3,0,2,1:T(8,128)S(1)} %get-tuple-element.234), channel_id=1, source_target_pairs={{1,0},{2,1},{3,2},{5,4},{6,5},{7,6},{9,8},{10,9},{11,10},{13,12},{... | collective-permute-start | bytes 294920 | tf_op jit(solution)/shard_map/ppermute | solution.py:25
  73.1 6.6 %collective-permute-start.16 = (f32[8,24,1,128]{3,0,2,1:T(8,128)S(1)}, f32[8,24,1,128]{3,0,2,1:T(8,128)S(1)}, u32[]{:S(2)}, u32[]{:S(2)}) collective-permute-start(f32[8,24,1,128]{3,0,2,1:T(8,128)S(1)} %get-tuple-element.235), channel_id=1, source_target_pairs={{0,1},{1,2},{2,3},{4,5},{5,6},{6,7},{8,9},{9,10},{10,11},{12,13},{... | collective-permute-start | bytes 294920 | tf_op jit(solution)/shard_map/ppermute | solution.py:24
  81.9 29.6 %collective-permute-start.17 = (f32[8,24,1,128]{3,0,2,1:T(8,128)S(1)}, f32[8,24,1,128]{3,0,2,1:T(8,128)S(1)}, u32[]{:S(2)}, u32[]{:S(2)}) collective-permute-start(f32[8,24,1,128]{3,0,2,1:T(8,128)S(1)} %get-tuple-element.230), channel_id=1, source_target_pairs={{1,0},{2,1},{3,2},{5,4},{6,5},{7,6},{9,8},{10,9},{11,10},{13,12},{... | collective-permute-start | bytes 294920 | tf_op jit(solution)/shard_map/ppermute | solution.py:25
  83.2 28.3 %collective-permute-start.18 = (f32[8,24,1,128]{3,0,2,1:T(8,128)S(1)}, f32[8,24,1,128]{3,0,2,1:T(8,128)S(1)}, u32[]{:S(2)}, u32[]{:S(2)}) collective-permute-start(f32[8,24,1,128]{3,0,2,1:T(8,128)S(1)} %get-tuple-element.231), channel_id=1, source_target_pairs={{0,1},{1,2},{2,3},{4,5},{5,6},{6,7},{8,9},{9,10},{10,11},{12,13},{... | collective-permute-start | bytes 294920 | tf_op jit(solution)/shard_map/ppermute | solution.py:24
where the time goes:
time: 115 us; the launch traced here: 114 us
  starting transfers between devices  61.9 us (54%)
  blocking collectives  21.8 us (19%)
  matrix products  10.8 us (9%)
  local copies, waits for them, and re-layouts  6.9 us (6%)
  other arithmetic  6.52 us (6%)
  waiting for transfers between devices  3.57 us (3%)
  between operations  2.42 us (2%)
    ppermute x9, starting transfers between devices, with_halo(): before = lax.ppermute(last, axis, up)  44.2 us
    psum x1, blocking collectives, per_device(): rate_grad = lax.psum(rate_term, 'tm') * scale  21.8 us
    ppermute x9, starting transfers between devices, with_halo(): after = lax.ppermute(leading, axis, down)  11.6 us
    ppermute x2, starting transfers between devices, shifted(): return lax.ppermute(block, axis, route)  6.09 us
    dot_general x4, matrix products, forward(): jnp.einsum('tu,ukln->tkln', bio_matrix, field, precision=lax.Precision.HI...  5.57 us
    dot_general x4, matrix products, per_device(): jnp.einsum('tu,tkln->ukln', bio_matrix, low, precision=lax.Precision.HIGH...  5.27 us
    unnamed x100, local copies, waits for them, and re-layouts  4.35 us
    unnamed x96, other arithmetic  3.86 us
  transfers between devices with their start and end apart: 20, of which 6 were waited for; matrix products, arithmetic and copies ran while one was open for 17% of the time, Pallas kernels for 0%

commit v1 on v0

v1 whole, which is shorter than its diff:
```python
import functools
import math

import jax
import jax.numpy as jnp
from jax import lax
from jax.experimental import pallas as pl
from jax.experimental.pallas import tpu as pltpu
from jax.sharding import PartitionSpec as P

STEPS = 4
CHUNK = 8
BODY = 4

lateral_mix = 0.24
bio_step = 0.25


def kernel(n_tm, n_sp, states, bio, rate, mixing, land, levels, out, rate_out,
           x, sweep, defect, follow, earlier, halo, depths, depth_halo, coef, diag, wets, rates,
           halo_send, halo_recv, depth_send, depth_recv,
           follow_send, follow_recv, defect_send, defect_recv, rate_send, rate_recv):
    tracers, depth = states.shape[1], states.shape[2]
    lons = states.shape[4]
    chunks = depth // CHUNK
    tm, sp = lax.axis_index("tm"), lax.axis_index("space")
    nxt, prv = lax.rem(tm + 1, n_tm), lax.rem(tm + n_tm - 1, n_tm)
    has_up, has_down = sp > 0, sp < n_sp - 1
    near = ((has_up, sp - 1, 0, 1), (has_down, sp + 1, 7, 0))

    barrier = pltpu.get_barrier_semaphore()
    for has, other, _, _ in near:
        @pl.when(has)
        def _():
            pl.semaphore_signal(barrier, inc=1, device_id={"space": other},
                                device_id_type=pl.DeviceIdType.MESH)
    for d in range(1, n_tm):
        pl.semaphore_signal(barrier, inc=1, device_id={"tm": lax.rem(tm + d, n_tm)},
                            device_id_type=pl.DeviceIdType.MESH)

    tile = (8, lons)
    row = lax.broadcasted_iota(jnp.int32, tile, 0)
    lane = lax.broadcasted_iota(jnp.int32, tile, 1)
    top, bottom = row == 0, row == 7
    first, last = lane == 0, lane == lons - 1

    depths[...] = jnp.where(land[...] == 1, levels[...], 0).astype(jnp.float32)
    own_depth = depths[...]

    def wet_of(depth_map, k):
        return jnp.where(jnp.asarray(k, jnp.int32).astype(jnp.float32) < depth_map, 1.0, 0.0)

    def mask(k, _):
        w = wet_of(own_depth, k)
        wets[k] = w
        for t in range(tracers):
            x[0, t, k] = states[0, t, k] * w
        return 0

    lax.fori_loop(0, depth, mask, 0)
    for side, has in ((0, has_up), (1, has_down)):
        @pl.when(jnp.logical_not(has))
        def _():
            depth_halo[side] = jnp.zeros(tile, jnp.float32)

            def blank(i, _):
                for t in range(tracers):
                    halo[i, side, t] = jnp.zeros(halo.shape[3:], jnp.float32)
                return 0
            lax.fori_loop(0, halo.shape[0], blank, 0)

    pl.semaphore_wait(barrier, n_tm - 1 + has_up.astype(jnp.int32) + has_down.astype(jnp.int32))

    def depth_copy(other, side):
        return pltpu.make_async_remote_copy(
            depths, depth_halo.at[side], depth_send.at[side], depth_recv.at[side],
            device_id={"space": other}, device_id_type=pl.DeviceIdType.MESH)

    def halo_copy(j, c, other, edge, side):
        part = pl.ds(c * CHUNK, CHUNK)
        return pltpu.make_async_remote_copy(
            x.at[j, :, part, pl.ds(edge, 1), :], halo.at[j, side, :, part],
            halo_send.at[j, c, side], halo_recv.at[j, c, side],
            device_id={"space": other}, device_id_type=pl.DeviceIdType.MESH)

    def send_halo(j, c):
        for has, other, edge, side in near:
            @pl.when(has)
            def _():
                halo_copy(j, c, other, edge, side).start()

    def wait_halo(j, c):
        for has, other, edge, side in near:
            @pl.when(has)
            def _():
                halo_copy(j, c, other, edge, 1 - side).wait_recv()

    def follow_copy(c):
        part = pl.ds(c * CHUNK, CHUNK)
        return pltpu.make_async_remote_copy(
            states.at[0, :, part], follow.at[:, part], follow_send.at[c], follow_recv.at[c],
            device_id={"tm": prv}, device_id_type=pl.DeviceIdType.MESH)

    def defect_copy(c):
        part = pl.ds(c * CHUNK, CHUNK)
        return pltpu.make_async_remote_copy(
            defect.at[:, part], earlier.at[:, part], defect_send.at[c], defect_recv.at[c],
            device_id={"tm": nxt}, device_id_type=pl.DeviceIdType.MESH)

    def rate_copy(d):
        return pltpu.make_async_remote_copy(
            rates.at[tm], rates.at[tm], rate_send.at[d - 1], rate_recv.at[d - 1],
            device_id={"tm": lax.rem(tm + d, n_tm)}, device_id_type=pl.DeviceIdType.MESH)

    for has, other, edge, side in near:
        @pl.when(has)
        def _():
            depth_copy(other, side).start()
    for c in range(chunks):
        send_halo(0, c)
    for c in range(chunks):
        follow_copy(c).start()

    one = jnp.ones(tile, jnp.float32)

    def couple(k):
        if k < 0 or k >= depth - 1:
            return jnp.zeros(tile, jnp.float32)
        return mixing[k] * wets[k] * wets[k + 1]

    gain = [one, one]
    for i in range(depth):
        for way in range(2):
            k = i if way == 0 else depth - 1 - i
            behind, ahead = (couple(k - 1), couple(k)) if way == 0 else (couple(k), couple(k - 1))
            inv = 1.0 / (gain[way] + ahead)
            forth = ahead * inv
            coef[way, 0, k] = lateral_mix * wets[k] * inv
            coef[way, 1, k] = behind * inv
            coef[way, 2, k] = forth
            gain[way] = 1.0 + forth * gain[way]

    for has, other, edge, side in near:
        @pl.when(has)
        def _():
            depth_copy(other, 1 - side).wait_recv()
    zero = jnp.zeros(tile, jnp.float32)
    up_depth = jnp.where(top, depth_halo[0, 7:8, :], pltpu.roll(own_depth, 1, 0))
    down_depth = jnp.where(bottom, depth_halo[1, 0:1, :], pltpu.roll(own_depth, 7, 0))
    west_depth = jnp.where(first, zero, pltpu.roll(own_depth, 1, 1))
    east_depth = jnp.where(last, zero, pltpu.roll(own_depth, lons - 1, 1))

    def diagonal(k, _):
        count = (wet_of(up_depth, k) + wet_of(down_depth, k)
                 + wet_of(west_depth, k) + wet_of(east_depth, k))
        diag[k] = 1.0 / lateral_mix - count
        return 0

    lax.fori_loop(0, depth, diagonal, 0)
    bio_rate = rate[...] * (bio_step / lateral_mix)

    def mixed_of(field, back):
        result = []
        for t in range(tracers):
            total = None
            for u in range(tracers):
                term = field[u] * (bio[u, t] if back else bio[t, u])
                total = term if total is None else total + term
            result.append(total)
        return result

    def beside(v):
        return (jnp.where(first, zero, pltpu.roll(v, 1, 1))
                + jnp.where(last, zero, pltpu.roll(v, lons - 1, 1)))

    def across(v, j, t, k):
        return (jnp.where(top, halo[j, 0, t, k], pltpu.roll(v, 1, 0))
                + jnp.where(bottom, halo[j, 1, t, k], pltpu.roll(v, 7, 0)))

    def levels_loop(c, way, body, carry):
        def several(i, carry):
            for b in range(BODY):
                s = i * BODY + b
                k = c * CHUNK + (s if way == 0 else CHUNK - 1 - s)
                carry = body(k, carry)
            return carry
        return lax.fori_loop(0, CHUNK // BODY, several, carry)

    def order(way):
        return range(chunks) if way == 0 else range(chunks - 1, -1, -1)

    zeros = (zero,) * tracers

    def eliminate(j, way, back, rate_term):
        def body(k, carry):
            prev, rate_term = carry
            field = [x[j, t, k] for t in range(tracers)]
            mixed = mixed_of(field, back)
            if back:
                for t in range(tracers):
                    rate_term = rate_term + mixed[t] * x[7 - j, t, k]
            a, b, d = coef[way, 0, k], coef[way, 1, k], diag[k]
            now = []
            for t in range(tracers):
                v = field[t]
                star = v * d + bio_rate * mixed[t] + (beside(v) + across(v, j, t, k))
                s = star * a + b * prev[t]
                sweep[t, k] = s
                now.append(s)
            return tuple(now), rate_term

        carry = (zeros, rate_term)
        for c in order(way):
            wait_halo(j, c)
            carry = levels_loop(c, way, body, carry)
        return carry[1]

    def substitute(j, way):
        def body(k, prev):
            e = coef[way, 2, k]
            now = []
            for t in range(tracers):
                s = sweep[t, k] + e * prev[t]
                x[j, t, k] = s
                now.append(s)
            return tuple(now)

        carry = zeros
        for c in order(1 - way):
            carry = levels_loop(c, 1 - way, body, carry)
            send_halo(j, c)

    rate_term = zero
    for j in range(STEPS):
        way = j % 2
        eliminate(j, way, False, zero)
        if j < STEPS - 1:
            substitute(j + 1, way)

    def turn(k, carry):
        prev, held = carry
        e, w = coef[1, 2, k], wets[k]
        a, b = coef[0, 0, k] * (1.0 / lateral_mix), coef[0, 1, k]
        ends, now = [], []
        for t in range(tracers):
            v = sweep[t, k] + e * prev[t]
            gap = v - w * follow[t, k]
            defect[t, k] = gap
            s = gap * a + b * held[t]
            sweep[t, k] = s
            ends.append(v)
            now.append(s)
        return tuple(ends), tuple(now)

    carry = (zeros, zeros)
    for c in range(chunks):
        follow_copy(c).wait_recv()
        carry = levels_loop(c, 0, turn, carry)
        defect_copy(c).start()
    substitute(STEPS, 0)

    for j in range(STEPS, 2 * STEPS - 1):
        way = (j + 1) % 2
        rate_term = eliminate(j, way, True, rate_term)
        substitute(j + 1, way)

    end = 2 * STEPS - 1

    def finish_inner(k, rate_term):
        field = [x[end, t, k] for t in range(tracers)]
        mixed = mixed_of(field, True)
        for t in range(tracers):
            rate_term = rate_term + mixed[t] * x[0, t, k]
        for t in range(tracers):
            sweep[t, k] = field[t] * diag[k] + bio_rate * mixed[t] + beside(field[t])
        return rate_term

    for c in range(chunks):
        rate_term = levels_loop(c, 0, finish_inner, rate_term)
    rates[tm] = rate_term
    for d in range(1, n_tm):
        rate_copy(d).start()

    def finish(k, carry):
        w = wets[k] * lateral_mix
        for t in range(tracers):
            v = x[end, t, k]
            out[0, t, k] = w * (sweep[t, k] + across(v, end, t, k)) - earlier[t, k]
        return carry

    for c in range(chunks):
        wait_halo(end, c)
        defect_copy(c).wait_recv()
        levels_loop(c, 0, finish, 0)

    for d in range(1, n_tm):
        origin = lax.rem(tm + n_tm - d, n_tm)
        pltpu.make_async_remote_copy(
            rates.at[tm], rates.at[origin], rate_send.at[d - 1], rate_recv.at[d - 1],
            device_id={"tm": origin}, device_id_type=pl.DeviceIdType.MESH).wait_recv()
    total = rates[0]
    for d in range(1, n_tm):
        total = total + rates[d]
    rate_out[...] = total * (bio_step / math.sqrt(STEPS * tracers * depth * n_tm))

    for has, other, edge, side in near:
        @pl.when(has)
        def _():
            depth_copy(other, side).wait_send()
            for j in range(2 * STEPS):
                for c in range(chunks):
                    halo_copy(j, c, other, edge, side).wait_send()
    for c in range(chunks):
        follow_copy(c).wait_send()
        defect_copy(c).wait_send()
    for d in range(1, n_tm):
        rate_copy(d).wait_send()


def per_device(states, bio_matrix, uptake_rate, mixing, land_sea, levels_active):
    n_tm, n_sp = lax.axis_size("tm"), lax.axis_size("space")
    _, tracers, depth, rows, lons = states.shape
    chunks = depth // CHUNK
    vmem = pl.BlockSpec(memory_space=pltpu.VMEM)
    smem = pl.BlockSpec(memory_space=pltpu.SMEM)
    field = (tracers, depth, rows, lons)
    f32 = jnp.float32
    dma = pltpu.SemaphoreType.DMA
    return pl.pallas_call(
        functools.partial(kernel, n_tm, n_sp),
        out_shape=(jax.ShapeDtypeStruct(states.shape, f32), jax.ShapeDtypeStruct(uptake_rate.shape, f32)),
        in_specs=[vmem, smem, vmem, vmem, vmem, vmem],
        out_specs=(vmem, vmem),
        scratch_shapes=[
            pltpu.VMEM((2 * STEPS,) + field, f32),
            pltpu.VMEM(field, f32),
            pltpu.VMEM(field, f32),
            pltpu.VMEM(field, f32),
            pltpu.VMEM(field, f32),
            pltpu.VMEM((2 * STEPS, 2, tracers, depth, 1, lons), f32),
            pltpu.VMEM((rows, lons), f32),
            pltpu.VMEM((2, rows, lons), f32),
            pltpu.VMEM((2, 3, depth, rows, lons), f32),
            pltpu.VMEM((depth, rows, lons), f32),
            pltpu.VMEM((depth, rows, lons), f32),
            pltpu.VMEM((n_tm, rows, lons), f32),
            dma((2 * STEPS, chunks, 2)), dma((2 * STEPS, chunks, 2)),
            dma((2,)), dma((2,)),
            dma((chunks,)), dma((chunks,)),
            dma((chunks,)), dma((chunks,)),
            dma((n_tm - 1,)), dma((n_tm - 1,)),
        ],
        compiler_params=pltpu.CompilerParams(
            collective_id=0, has_side_effects=True, vmem_limit_bytes=40 * 1024 * 1024),
    )(states, bio_matrix, uptake_rate, mixing, land_sea, levels_active)


def solution(mesh):
    return jax.shard_map(
        per_device,
        mesh=mesh,
        in_specs=(
            P("tm", None, None, "space", None),
            P(),
            P("space", None),
            P(None, "space", None),
            P("space", None),
            P("space", None),
        ),
        out_specs=(P("tm", None, None, "space", None), P("space", None)),
        check_vma=False,
    )
```

time: 115 us -> 64.1 us (0.56)
  starting transfers between devices: 61.9 us -> 0 us
  Pallas kernels: 0 us -> 56.4 us
  blocking collectives: 21.8 us -> 0 us
  matrix products: 10.8 us -> 0 us
  other arithmetic: 6.52 us -> 0 us
  waiting for transfers between devices: 3.57 us -> 0 us
  between operations: 2.42 us -> 0.65 us
    ppermute x20 -> x0, starting transfers between devices: 61.9 us -> none  [the longest x9 44.2 us: with_halo(): before = lax.ppermute(last, axis, up)]
    pallas_call x0 -> x1, Pallas kernels: none -> 56.4 us  [per_device(): pl.pallas_call(functools.partial(kernel, n_tm, n_sp), out_shape=(jax.Shap...]
    psum x1 -> x0, blocking collectives: 21.8 us -> none  [per_device(): rate_grad = lax.psum(rate_term, 'tm') * scale]
    dot_general x8 -> x0, matrix products: 10.8 us -> none  [the longest x4 5.57 us: forward(): jnp.einsum('tu,ukln->tkln', bio_matrix, field, precision=lax.Precision.HI...]
    unnamed x96 -> x0, other arithmetic: 3.86 us -> none
    ppermute x20 -> x0, waiting for transfers between devices: 3.57 us -> none  [the longest x9 3.54 us: with_halo(): before = lax.ppermute(last, axis, up)]
    slice x18 -> x0, local copies, waits for them, and re-layouts: 2.55 us -> none  [the longest x9 2.41 us: shift_cols(): east_val = jnp.concatenate([field[..., 1:], zero_col], axis=-1)]
    unnamed x100 -> x14, local copies, waits for them, and re-layouts: 4.35 us -> 6.24 us
  transfers between devices with their start and end apart: 20 -> 0, of which waited for: 6 -> 0; matrix products, arithmetic and copies ran while one was open for 17% -> 0% of each run, Pallas kernels for 0% -> 0%
where the time goes in v1:
time: 64.1 us; the launch traced here: 63.3 us
  Pallas kernels  56.4 us (88%)
  local copies, waits for them, and re-layouts  6.24 us (10%)
  between operations  0.65 us (1%)
    pallas_call x1, Pallas kernels, per_device(): pl.pallas_call(functools.partial(kernel, n_tm, n_sp), out_shape=(jax.Shap...  56.4 us
    unnamed x14, local copies, waits for them, and re-layouts  6.24 us

profile of v1, /device:TPU:0, one launch (start us, length us, event | category | flops | bytes accessed | tf_op | source)
XLA Modules:
  0.0 63.3 jit_solution(5202316069947410416)
XLA Ops:
  0.6 0.0 copy-start
  0.6 1.1 %copy-done = f32[1,8,24,8,128]{4,3,2,1,0:T(8,128)S(1)} copy-done((f32[1,8,24,8,128]{4,3,2,1,0:T(8,128)S(1)}, f32[1,8,24,8,128]{4,3,2,1,0:T(8,128)}, u32[]{:S(2)}) %copy-start) | copy-done | bytes 786456
  1.8 0.0 copy-start.1
  1.8 0.9 %copy-done.1 = f32[23,8,128]{2,1,0:T(8,128)S(1)} copy-done((f32[23,8,128]{2,1,0:T(8,128)S(1)}, f32[23,8,128]{2,1,0:T(8,128)}, u32[]{:S(2)}) %copy-start.1) | copy-done | bytes 94232
  2.7 0.0 copy-start.2
  2.7 0.7 %copy-done.2 = f32[8,8]{1,0:T(8,128)S(1)} copy-done((f32[8,8]{1,0:T(8,128)S(1)}, f32[8,8]{1,0:T(8,128)}, u32[]{:S(2)}) %copy-start.2) | copy-done | bytes 280
  3.3 0.0 copy-start.3
  3.3 0.7 %copy-done.3 = f32[8,128]{1,0:T(8,128)S(1)} copy-done((f32[8,128]{1,0:T(8,128)S(1)}, f32[8,128]{1,0:T(8,128)}, u32[]{:S(2)}) %copy-start.3) | copy-done | bytes 4120
  4.0 0.0 copy-start.4
  4.0 0.7 %copy-done.4 = s32[8,128]{1,0:T(8,128)S(1)} copy-done((s32[8,128]{1,0:T(8,128)S(1)}, s32[8,128]{1,0:T(8,128)}, u32[]{:S(2)}) %copy-start.4) | copy-done | bytes 4120
  4.7 0.0 copy-start.5
  4.7 0.7 %copy-done.5 = s32[8,128]{1,0:T(8,128)S(1)} copy-done((s32[8,128]{1,0:T(8,128)S(1)}, s32[8,128]{1,0:T(8,128)}, u32[]{:S(2)}) %copy-start.5) | copy-done | bytes 4120
  5.4 56.4 %shard_map.77 = (f32[1,8,24,8,128]{4,3,2,1,0:T(8,128)S(1)}, f32[8,128]{1,0:T(8,128)S(1)}) custom-call(f32[1,8,24,8,128]{4,3,2,1,0:T(8,128)S(1)} %copy-done, f32[8,8]{1,0:T(8,128)S(1)} %copy-done.2, f32[8,128]{1,0:T(8,128)S(1)} %copy-done.3, f32[23,8,128]{2,1,0:T(8,128)S(1)} %copy-done.1, s32[8,128]{1,0:T(8,128)S(1)} %copy-done.4, s32[8,128]{1,0:T(8,128)S(1)} %copy-done.5), custom_call_target="tpu_custom_call" | custom-call | tf_op jit(solution)/shard_map/pallas_call | solution.py:329
  61.9 0.9 %copy.10 = f32[1,8,24,8,128]{4,3,2,1,0:T(8,128)} copy(f32[1,8,24,8,128]{4,3,2,1,0:T(8,128)S(1)} %get-tuple-element.4) | data formatting | bytes 1572864
  62.7 0.6 copy.11
Async XLA Ops:
  0.6 1.1 %copy-start = (f32[1,8,24,8,128]{4,3,2,1,0:T(8,128)S(1)}, f32[1,8,24,8,128]{4,3,2,1,0:T(8,128)}, u32[]{:S(2)}) copy-start(f32[1,8,24,8,128]{4,3,2,1,0:T(8,128)} %states.1) | copy-start | bytes 2359300
  1.8 0.9 %copy-start.1 = (f32[23,8,128]{2,1,0:T(8,128)S(1)}, f32[23,8,128]{2,1,0:T(8,128)}, u32[]{:S(2)}) copy-start(f32[23,8,128]{2,1,0:T(8,128)} %mixing.1) | copy-start | bytes 282628
  2.7 0.7 %copy-start.2 = (f32[8,8]{1,0:T(8,128)S(1)}, f32[8,8]{1,0:T(8,128)}, u32[]{:S(2)}) copy-start(f32[8,8]{1,0:T(8,128)} %bio.1) | copy-start | bytes 772
  3.3 0.7 %copy-start.3 = (f32[8,128]{1,0:T(8,128)S(1)}, f32[8,128]{1,0:T(8,128)}, u32[]{:S(2)}) copy-start(f32[8,128]{1,0:T(8,128)} %rate.1) | copy-start | bytes 12292
  4.0 0.7 %copy-start.4 = (s32[8,128]{1,0:T(8,128)S(1)}, s32[8,128]{1,0:T(8,128)}, u32[]{:S(2)}) copy-start(s32[8,128]{1,0:T(8,128)} %land.1) | copy-start | bytes 12292
  4.7 0.7 %copy-start.5 = (s32[8,128]{1,0:T(8,128)S(1)}, s32[8,128]{1,0:T(8,128)}, u32[]{:S(2)}) copy-start(s32[8,128]{1,0:T(8,128)} %levels.1) | copy-start | bytes 12292
